TPU v7x, 512 devices: a whole 4x4x16 slice. The times are simulated.
512 devices in a mesh: grp: 16 (over x, y_hi, core), seq: 32 (over z, y_lo).
Axes of the slice: x: 4, y: 4 (y_hi: 2, y_lo: 2; y = y_hi * 2 + y_lo), z: 16, core: 2. Of those that a mesh axis runs over, the one named last changes fastest.
Arguments:
- query_vectors: bfloat16 [512, 256, 2048], P(('grp', 'seq')), parts along dimension 0, may hold values from -4000 to 4000
- key_vectors: bfloat16 [512, 256, 2048], P(('grp', 'seq')), parts along dimension 0, may hold values from -6 to 6
- value_vectors: bfloat16 [512, 256, 2048], P(('grp', 'seq')), parts along dimension 0, may hold values from -6 to 6
Outputs:
- attended: bfloat16 [512, 256, 2048], P(('grp', 'seq')), parts along dimension 0
There are 16 independent parts, one for each index of `grp`. A program takes and returns all parts, laid end to end along the dimension named above; each array names one. Nothing has to cross between parts.
All inputs are finite; a program needn't handle non-finite values.
Results may differ from a plain program's by a relative error of at most 0.0065.
Values may be sent and summed in bfloat16 or wider, within the bound.
A program may use at most 64 MiB of HBM per device.

v0:
```python
import math

import jax
import jax.numpy as jnp
from jax import lax
from jax.sharding import PartitionSpec as P

HEADS = 16
HD = 128


floor_score = -1e30


def attend(query_vectors, key_vectors, value_vectors, allowed, layout):
    shape = query_vectors.shape
    split = (shape[0], shape[1], shape[2] // HD, HD)
    query_heads = query_vectors.reshape(split)
    key_heads = key_vectors.reshape(split)
    value_heads = value_vectors.reshape(split)
    if layout == "rows":
        score_form, blend_form, order = ("rahd,rbhd->rhab", "rhab,rbhd->rahd", (0, 2, 1))
    else:
        score_form, blend_form, order = ("arhd,brhd->rhab", "rhab,brhd->arhd", (2, 0, 1))
    scores = jnp.einsum(score_form, query_heads, key_heads, preferred_element_type=jnp.float32) * (
        1.0 / math.sqrt(HD)
    )
    scores = jnp.where(allowed, scores, floor_score)
    highest = jnp.max(scores, axis=3)
    weights = jnp.where(allowed, jnp.exp(scores - highest[..., None]), 0.0)
    totals = jnp.sum(weights, axis=3)
    blend = jnp.einsum(
        blend_form, weights.astype(jnp.bfloat16), value_heads, preferred_element_type=jnp.float32
    )
    return (
        blend.reshape(shape).astype(jnp.bfloat16),
        jnp.transpose(highest, order),
        jnp.transpose(totals, order),
    )


def combine_parts(row_out, row_high, row_total, col_out, col_high, col_total):
    highest = jnp.maximum(row_high, col_high)
    row_factor = jnp.exp(row_high - highest)
    col_factor = jnp.exp(col_high - highest)
    split = row_out.shape[:-1] + (HEADS, HD)
    numer = row_out.astype(jnp.float32).reshape(split) * row_factor[..., None]
    numer = numer + col_out.astype(jnp.float32).reshape(split) * col_factor[..., None]
    denom = row_total * row_factor + col_total * col_factor
    return (numer / denom[..., None]).reshape(row_out.shape).astype(jnp.bfloat16)


def local(query_vectors, key_vectors, value_vectors):
    rows_local, columns, width = query_vectors.shape
    all_rows = rows_local * lax.axis_size("seq")
    col_index = jnp.arange(columns, dtype=jnp.int32)
    row_allowed = col_index[None, :] <= col_index[:, None]
    row_index = jnp.arange(all_rows, dtype=jnp.int32)
    col_allowed = row_index[None, :] < row_index[:, None]
    row_out, row_high, row_total = attend(
        query_vectors, key_vectors, value_vectors, row_allowed, "rows"
    )
    moved = (
        lax.all_to_all(query_vectors, "seq", split_axis=1, concat_axis=0, tiled=True),
        lax.all_to_all(key_vectors, "seq", split_axis=1, concat_axis=0, tiled=True),
        lax.all_to_all(value_vectors, "seq", split_axis=1, concat_axis=0, tiled=True),
        lax.all_to_all(row_out, "seq", split_axis=1, concat_axis=0, tiled=True),
    )
    moved_high, moved_total = (
        lax.all_to_all(row_high, "seq", split_axis=1, concat_axis=0, tiled=True),
        lax.all_to_all(row_total, "seq", split_axis=1, concat_axis=0, tiled=True),
    )
    col_out, col_high, col_total = attend(moved[0], moved[1], moved[2], col_allowed, "cols")
    finished = combine_parts(moved[3], moved_high, moved_total, col_out, col_high, col_total)
    return lax.all_to_all(finished, "seq", split_axis=0, concat_axis=1, tiled=True)


def solution(mesh):
    in_specs = (
        P(("grp", "seq"), None, None),
        P(("grp", "seq"), None, None),
        P(("grp", "seq"), None, None),
    )
    out_specs = P(("grp", "seq"), None, None)
    return jax.shard_map(local, mesh=mesh, in_specs=in_specs, out_specs=out_specs, check_vma=False)
```

profile of v0, /device:TPU:1, one launch (start us, length us, event | category | flops | bytes accessed | tf_op | source)
XLA Modules:
  0.0 369.9 jit_solution(14358664335463258626)
XLA Ops:
  0.0 1.5 copy.49
  1.6 0.2 copy.50
  1.8 1.0 fusion
  2.9 0.0 copy-start.2
  2.9 1.0 fusion.1
  3.9 1.0 copy-done.6
  4.9 0.1 copy.43
  5.0 0.6 broadcast.19
  5.6 1.0 reduce.14
  6.6 0.7 reshape.111
  7.3 17.0 %all-to-all-start.5 = ((f32[32,1,128]{2,1,0:T(1,128)}), f32[32,1,128]{2,1,0:T(1,128)S(1)}, u32[]{:S(2)}, u32[]{:S(2)}) async-start(f32[32,1,128]{2,1,0:T(1,128)} %reshape.111), calls=%async_computation.5 | async-start | bytes 32768 | tf_op jit(solution)/shard_map/all_to_all | solution.py:71
  24.3 0.1 copy.32
  24.4 1.0 reduce.16
  25.5 0.7 reshape.109
  26.2 10.2 %all-to-all-done.5 = f32[32,1,128]{2,1,0:T(1,128)S(1)} async-done(((f32[32,1,128]{2,1,0:T(1,128)}), f32[32,1,128]{2,1,0:T(1,128)S(1)}, u32[]{:S(2)}, u32[]{:S(2)}) %all-to-all-start.5) | async-done | bytes 16416 | tf_op jit(solution)/shard_map/all_to_all | solution.py:71
  36.3 4.2 %all-to-all-start.1 = ((f32[32,1,128]{2,1,0:T(1,128)}), f32[32,1,128]{2,1,0:T(1,128)S(1)}, u32[]{:S(2)}, u32[]{:S(2)}) async-start(f32[32,1,128]{2,1,0:T(1,128)} %reshape.109), calls=%async_computation.1 | async-start | bytes 32768 | tf_op jit(solution)/shard_map/all_to_all | solution.py:70
  40.6 1.6 copy.84
  42.2 0.5 broadcast.15
  42.7 7.7 %reduce.12 = bf16[256,2048]{1,0:T(8,128)(2,1)} reduce(bf16[256,1,2048]{2,1,0:T(2,128)(2,1)S(1)} %bitcast.79, bf16[]{:T(256)} %broadcast.15), dimensions={1}, to_apply=%bitcast.78.reduce_sub_computation | reduce | bytes 2097154
  50.4 3.0 reshape.105
  53.4 12.9 %all-to-all-start.2 = ((bf16[32,2,8192]{2,1,0:T(2,128)(2,1)}), bf16[32,2,8192]{2,1,0:T(2,128)(2,1)}, u32[]{:S(2)}, u32[]{:S(2)}) async-start(bf16[32,2,8192]{2,1,0:T(2,128)(2,1)} %reshape.105), calls=%async_computation.2 | async-start | bytes 2097152 | tf_op jit(solution)/shard_map/all_to_all | solution.py:64
  66.4 1.6 copy.83
  68.0 7.7 %reduce.11 = bf16[256,2048]{1,0:T(8,128)(2,1)} reduce(bf16[256,1,2048]{2,1,0:T(2,128)(2,1)S(1)} %bitcast.82, bf16[]{:T(256)} %broadcast.15), dimensions={1}, to_apply=%bitcast.77.reduce_sub_computation | reduce | bytes 2097154
  75.7 3.0 reshape.103
  78.7 39.3 %all-to-all-done.2 = bf16[32,2,8192]{2,1,0:T(2,128)(2,1)} async-done(((bf16[32,2,8192]{2,1,0:T(2,128)(2,1)}), bf16[32,2,8192]{2,1,0:T(2,128)(2,1)}, u32[]{:S(2)}, u32[]{:S(2)}) %all-to-all-start.2) | async-done | bytes 1048608 | tf_op jit(solution)/shard_map/all_to_all | solution.py:64
  118.0 7.0 %all-to-all-start.3 = ((bf16[32,2,8192]{2,1,0:T(2,128)(2,1)}), bf16[32,2,8192]{2,1,0:T(2,128)(2,1)}, u32[]{:S(2)}, u32[]{:S(2)}) async-start(bf16[32,2,8192]{2,1,0:T(2,128)(2,1)} %reshape.103), calls=%async_computation.3 | async-start | bytes 2097152 | tf_op jit(solution)/shard_map/all_to_all | solution.py:65
  125.0 0.5 copy.48
  125.5 4.3 %fusion.14 = bf16[16,256,128]{1,2,0:T(8,128)(2,1)} fusion(bf16[256,16,128]{0,2,1:T(8,128)(2,1)S(1)} %bitcast.93, f32[16,256,256]{1,2,0:T(8,128)} %copy-done.6, f32[16,256]{1,0:T(8,128)S(1)} %get-tuple-element.8, pred[256,256]{0,1:T(8,128)(4,1)S(1)} %iota_compare_fusion), kind=kOutput, calls=%fused_computation.19 | convolution fusion | flops 274202624 | bytes 6373376 | tf_op jit(solution)/shard_map/rhab,rbhd->rahd/dot_general | solution.py:32
  129.8 4.7 %copy.31 = bf16[1,256,2048]{2,0,1:T(2,128)(2,1)S(1)} copy(bf16[1,256,2048]{1,2,0:T(8,128)(2,1)} %bitcast.90) | data formatting | bytes 2097152 | tf_op jit(solution)/shard_map/convert_element_type | solution.py:36
  134.6 7.7 %reduce.10 = bf16[256,2048]{1,0:T(8,128)(2,1)} reduce(bf16[256,1,2048]{2,1,0:T(2,128)(2,1)S(1)} %bitcast.80, bf16[]{:T(256)} %broadcast.15), dimensions={1}, to_apply=%bitcast.53.reduce_sub_computation | reduce | bytes 2097154
  142.2 3.0 reshape.101
  145.2 31.5 %all-to-all-done.3 = bf16[32,2,8192]{2,1,0:T(2,128)(2,1)} async-done(((bf16[32,2,8192]{2,1,0:T(2,128)(2,1)}), bf16[32,2,8192]{2,1,0:T(2,128)(2,1)}, u32[]{:S(2)}, u32[]{:S(2)}) %all-to-all-start.3) | async-done | bytes 1048608 | tf_op jit(solution)/shard_map/all_to_all | solution.py:65
  176.6 7.1 %all-to-all-start = ((bf16[32,2,8192]{2,1,0:T(2,128)(2,1)}), bf16[32,2,8192]{2,1,0:T(2,128)(2,1)}, u32[]{:S(2)}, u32[]{:S(2)}) async-start(bf16[32,2,8192]{2,1,0:T(2,128)(2,1)} %reshape.101), calls=%async_computation | async-start | bytes 2097152 | tf_op jit(solution)/shard_map/all_to_all | solution.py:67
  183.8 1.6 copy.82
  185.4 6.7 %reduce.13 = bf16[256,2048]{1,0:T(8,128)(2,1)S(1)} reduce(bf16[256,1,2048]{2,1,0:T(2,128)(2,1)S(1)} %bitcast.81, bf16[]{:T(256)} %broadcast.15), dimensions={1}, to_apply=%bitcast.76.reduce_sub_computation | reduce | bytes 2097154
  192.1 1.9 reshape.107
  194.0 41.4 %all-to-all-done = bf16[32,2,8192]{2,1,0:T(2,128)(2,1)} async-done(((bf16[32,2,8192]{2,1,0:T(2,128)(2,1)}), bf16[32,2,8192]{2,1,0:T(2,128)(2,1)}, u32[]{:S(2)}, u32[]{:S(2)}) %all-to-all-start) | async-done | bytes 1048608 | tf_op jit(solution)/shard_map/all_to_all | solution.py:67
  235.5 6.6 %all-to-all-start.4 = ((bf16[32,2,8192]{2,1,0:T(2,128)(2,1)}), bf16[32,2,8192]{2,1,0:T(2,128)(2,1)S(1)}, u32[]{:S(2)}, u32[]{:S(2)}) async-start(bf16[32,2,8192]{2,1,0:T(2,128)(2,1)} %reshape.107), calls=%async_computation.4 | async-start | bytes 2097152 | tf_op jit(solution)/shard_map/all_to_all | solution.py:66
  242.1 0.7 reduce.15
  242.8 0.2 reshape.112
  243.0 0.1 copy.44
  243.1 0.7 reduce.17
  243.9 0.2 reshape.110
  244.1 0.1 copy.38
  244.2 4.3 %reshape.106 = bf16[256,1,2048]{2,1,0:T(2,128)(2,1)S(1)} reshape(bf16[32,2,8192]{2,1,0:T(2,128)(2,1)} %all-to-all-done.2) | data formatting | bytes 2097152
  248.6 5.8 %reshape.104 = bf16[256,1,2048]{2,1,0:T(2,128)(2,1)} reshape(bf16[32,2,8192]{2,1,0:T(2,128)(2,1)} %all-to-all-done.3) | data formatting | bytes 2097152
  254.4 6.0 %reshape.102 = bf16[256,1,2048]{2,1,0:T(2,128)(2,1)} reshape(bf16[32,2,8192]{2,1,0:T(2,128)(2,1)} %all-to-all-done) | data formatting | bytes 2097152
  260.3 7.1 %bitcast_reduce_fusion.1 = bf16[256,2048]{1,0:T(8,128)(2,1)} fusion(bf16[256,1,2048]{2,1,0:T(2,128)(2,1)S(1)} %reshape.106), kind=kLoop, calls=%fused_computation.53 | loop fusion | bytes 2097152 | tf_op jit(solution)/shard_map/all_to_all | solution.py:64
  267.4 7.3 %bitcast_reduce_fusion.2 = bf16[256,2048]{1,0:T(8,128)(2,1)} fusion(bf16[256,1,2048]{2,1,0:T(2,128)(2,1)S(1)} %copy-done), kind=kLoop, calls=%fused_computation.54 | loop fusion | bytes 2097152 | tf_op jit(solution)/shard_map/all_to_all | solution.py:65
  274.7 3.5 bitcast_convert_fusion
  278.1 15.7 %all-to-all-done.4 = bf16[32,2,8192]{2,1,0:T(2,128)(2,1)S(1)} async-done(((bf16[32,2,8192]{2,1,0:T(2,128)(2,1)}), bf16[32,2,8192]{2,1,0:T(2,128)(2,1)S(1)}, u32[]{:S(2)}, u32[]{:S(2)}) %all-to-all-start.4) | async-done | bytes 1048608 | tf_op jit(solution)/shard_map/all_to_all | solution.py:66
  293.8 1.0 reshape.108
  294.9 0.0 copy-start.8
  294.9 6.1 %bitcast_reduce_fusion = bf16[256,2048]{1,0:T(8,128)(2,1)S(1)} fusion(bf16[256,1,2048]{2,1,0:T(2,128)(2,1)S(1)} %reshape.108), kind=kLoop, calls=%fused_computation.52 | loop fusion | bytes 2097152 | tf_op jit(solution)/shard_map/all_to_all | solution.py:66
  301.0 0.2 copy.81
  301.2 0.6 copy_bitcast_fusion.1
  301.9 1.7 fusion.13
  303.6 0.8 fusion.17
  304.5 0.7 copy-done.9
  305.2 2.8 fusion.7
  308.0 0.4 copy.45
  308.5 0.5 convert_element_type.68
  309.0 59.7 %all_to_all.72 = bf16[32,8,2048]{2,1,0:T(8,128)(2,1)S(1)} all-to-all(bf16[32,8,2048]{2,1,0:T(8,128)(2,1)S(1)} %convert_element_type.68), channel_id=1, replica_groups=mesh['grp'=16,'seq'=32] {'seq'}, dimensions={0} | all-to-all | bytes 2097152 | tf_op jit(solution)/shard_map/all_to_all | solution.py:75
  368.7 1.0 copy.86
  (20 shorter events, 0.1 us)
Async XLA Ops:
  0.0 1.6 copy-start.3
  2.9 2.0 copy-start.6
  2.9 37.7 %copy-start.2 = (bf16[1,256,2048]{2,1,0:T(8,128)(2,1)S(1)}, bf16[1,256,2048]{2,1,0:T(8,128)(2,1)}, u32[]{:S(2)}) copy-start(bf16[1,256,2048]{2,1,0:T(8,128)(2,1)} %param.3) | copy-start | bytes 3145732
  7.3 29.0 %all-to-all-start.5 = ((f32[32,1,128]{2,1,0:T(1,128)}), f32[32,1,128]{2,1,0:T(1,128)S(1)}, u32[]{:S(2)}, u32[]{:S(2)}) async-start(f32[32,1,128]{2,1,0:T(1,128)} %reshape.111), calls=%async_computation.5 | async-start | bytes 32768 | tf_op jit(solution)/shard_map/all_to_all | solution.py:71
  36.3 17.1 %all-to-all-start.1 = ((f32[32,1,128]{2,1,0:T(1,128)}), f32[32,1,128]{2,1,0:T(1,128)S(1)}, u32[]{:S(2)}, u32[]{:S(2)}) async-start(f32[32,1,128]{2,1,0:T(1,128)} %reshape.109), calls=%async_computation.1 | async-start | bytes 32768 | tf_op jit(solution)/shard_map/all_to_all | solution.py:70
  50.4 16.0 %copy-start.4 = (bf16[1,256,2048]{2,1,0:T(8,128)(2,1)S(1)}, bf16[1,256,2048]{2,1,0:T(8,128)(2,1)}, u32[]{:S(2)}) copy-start(bf16[1,256,2048]{2,1,0:T(8,128)(2,1)} %param.4) | copy-start | bytes 3145732
  53.4 64.6 %all-to-all-start.2 = ((bf16[32,2,8192]{2,1,0:T(2,128)(2,1)}), bf16[32,2,8192]{2,1,0:T(2,128)(2,1)}, u32[]{:S(2)}, u32[]{:S(2)}) async-start(bf16[32,2,8192]{2,1,0:T(2,128)(2,1)} %reshape.105), calls=%async_computation.2 | async-start | bytes 2097152 | tf_op jit(solution)/shard_map/all_to_all | solution.py:64
  75.7 49.3 %copy-start.5 = (bf16[1,256,2048]{2,1,0:T(8,128)(2,1)S(1)}, bf16[1,256,2048]{2,1,0:T(8,128)(2,1)}, u32[]{:S(2)}) copy-start(bf16[1,256,2048]{2,1,0:T(8,128)(2,1)} %param.5) | copy-start | bytes 3145732
  118.0 58.7 %all-to-all-start.3 = ((bf16[32,2,8192]{2,1,0:T(2,128)(2,1)}), bf16[32,2,8192]{2,1,0:T(2,128)(2,1)}, u32[]{:S(2)}, u32[]{:S(2)}) async-start(bf16[32,2,8192]{2,1,0:T(2,128)(2,1)} %reshape.103), calls=%async_computation.3 | async-start | bytes 2097152 | tf_op jit(solution)/shard_map/all_to_all | solution.py:65
  176.6 58.8 %all-to-all-start = ((bf16[32,2,8192]{2,1,0:T(2,128)(2,1)}), bf16[32,2,8192]{2,1,0:T(2,128)(2,1)}, u32[]{:S(2)}, u32[]{:S(2)}) async-start(bf16[32,2,8192]{2,1,0:T(2,128)(2,1)} %reshape.101), calls=%async_computation | async-start | bytes 2097152 | tf_op jit(solution)/shard_map/all_to_all | solution.py:67
  235.5 58.4 %all-to-all-start.4 = ((bf16[32,2,8192]{2,1,0:T(2,128)(2,1)}), bf16[32,2,8192]{2,1,0:T(2,128)(2,1)S(1)}, u32[]{:S(2)}, u32[]{:S(2)}) async-start(bf16[32,2,8192]{2,1,0:T(2,128)(2,1)} %reshape.107), calls=%async_computation.4 | async-start | bytes 2097152 | tf_op jit(solution)/shard_map/all_to_all | solution.py:66
  260.3 7.1 %copy-start = (bf16[256,1,2048]{2,1,0:T(2,128)(2,1)S(1)}, bf16[256,1,2048]{2,1,0:T(2,128)(2,1)}, u32[]{:S(2)}) copy-start(bf16[256,1,2048]{2,1,0:T(2,128)(2,1)} %reshape.104) | copy-start | bytes 3145732
  267.4 7.3 %copy-start.1 = (bf16[256,1,2048]{2,1,0:T(2,128)(2,1)S(1)}, bf16[256,1,2048]{2,1,0:T(2,128)(2,1)}, u32[]{:S(2)}) copy-start(bf16[256,1,2048]{2,1,0:T(2,128)(2,1)} %reshape.102) | copy-start | bytes 3145732
  294.9 6.3 %copy-start.7 = (bf16[256,2048]{1,0:T(8,128)(2,1)S(1)}, bf16[256,2048]{1,0:T(8,128)(2,1)}, u32[]{:S(2)}) copy-start(bf16[256,2048]{1,0:T(8,128)(2,1)} %bitcast_reduce_fusion.1) | copy-start | bytes 3145732
  294.9 6.3 %copy-start.8 = (bf16[256,2048]{1,0:T(8,128)(2,1)S(1)}, bf16[256,2048]{1,0:T(8,128)(2,1)}, u32[]{:S(2)}) copy-start(bf16[256,2048]{1,0:T(8,128)(2,1)} %bitcast_reduce_fusion.2) | copy-start | bytes 3145732
  303.6 1.6 copy-start.9
where the time goes:
time: 375 us; the launch traced here: 370 us
  waiting for transfers between devices  138 us (37%)
  local copies, waits for them, and re-layouts  68.2 us (18%)
  blocking collectives  59.7 us (16%)
  starting transfers between devices  54.9 us (15%)
  other arithmetic  38.6 us (10%)
  matrix products  9.89 us (3%)
    all_to_all x1, blocking collectives, local(): lax.all_to_all(finished, 'seq', split_axis=0, concat_axis=1, tiled=True)  59.7 us
    all_to_all x1, waiting for transfers between devices, local(): lax.all_to_all(row_out, 'seq', split_axis=1, concat_axis=0, tiled=True)  41.4 us
    unnamed x41, local copies, waits for them, and re-layouts  40.6 us
    all_to_all x1, waiting for transfers between devices, local(): lax.all_to_all(query_vectors, 'seq', split_axis=1, concat_axis=0, tiled=T...  39.3 us
    unnamed x6, other arithmetic  31.8 us
    all_to_all x1, waiting for transfers between devices, local(): lax.all_to_all(key_vectors, 'seq', split_axis=1, concat_axis=0, tiled=True)  31.5 us
    all_to_all x1, starting transfers between devices, local(): lax.all_to_all(row_total, 'seq', split_axis=1, concat_axis=0, tiled=True)  17 us
    all_to_all x1, waiting for transfers between devices, local(): lax.all_to_all(value_vectors, 'seq', split_axis=1, concat_axis=0, tiled=T...  15.7 us
  transfers between devices with their start and end apart: 6, of which 5 were waited for; matrix products, arithmetic and copies ran while one was open for 25% of the time, Pallas kernels for 0%

commit v1 on v0

v1 whole, which is shorter than its diff:
```python
import functools
import math

import jax
import jax.numpy as jnp
from jax import lax
from jax.experimental import pallas as pl
from jax.experimental.pallas import tpu as pltpu
from jax.sharding import PartitionSpec as P

HEADS = 16
HD = 128
FLOOR = -1e30
POWER = math.log2(math.e) / math.sqrt(HD)
CHUNK_HEADS = 4
MESH = pl.DeviceIdType.MESH


def attend(queries, keys, values, bias):
    scores = lax.dot_general(
        queries, keys, (((1,), (1,)), ((), ())), preferred_element_type=jnp.float32
    )
    scores = scores + bias
    high = jnp.max(scores, axis=1, keepdims=True)
    weights = jnp.exp2((scores - high) * POWER)
    total = jnp.sum(weights, axis=1, keepdims=True)
    out = jnp.dot(weights.astype(jnp.bfloat16), values, preferred_element_type=jnp.float32)
    return out, high, total


def kernel(
    n, cols,
    q_ref, k_ref, v_ref, out_ref,
    q_all, k_all, v_all, back, home, row_out, row_stats, col_stats, home_stats, row_bias, col_bias,
    send_sem, recv_sem, back_send, back_recv, stat_send, stat_recv, own_sem,
):
    me = lax.axis_index("seq")
    width = CHUNK_HEADS * HD
    chunks = HEADS // CHUNK_HEADS
    tokens = n * cols
    forward = ((q_ref, q_all), (k_ref, k_all), (v_ref, v_all))

    def peer(step):
        return lax.rem(me + step, n)

    barrier = pltpu.get_barrier_semaphore()

    def greet(step, carry):
        pl.semaphore_signal(
            barrier, inc=1, device_id={"seq": peer(step)}, device_id_type=MESH
        )
        return carry

    lax.fori_loop(1, n, greet, 0)

    own = [
        pltpu.make_async_copy(src.at[me], dst.at[me], own_sem.at[i])
        for i, (src, dst) in enumerate(forward)
    ]
    for copy in own:
        copy.start()

    index = lax.broadcasted_iota(jnp.int32, (tokens, tokens), 0)
    other = lax.broadcasted_iota(jnp.int32, (tokens, tokens), 1)
    row_bias[...] = jnp.where(other <= index, 0.0, FLOOR)
    same = lax.rem(index, cols) == lax.rem(other, cols)
    before = lax.div(other, cols) < lax.div(index, cols)
    col_bias[...] = jnp.where(same & before, 0.0, FLOOR)

    pl.semaphore_wait(barrier, n - 1)

    def lanes(chunk):
        return pl.ds(chunk * width, width)

    def send_chunk(chunk):
        def send(step, carry):
            to = peer(step)
            for i, (src, dst) in enumerate(forward):
                pltpu.make_async_remote_copy(
                    src_ref=src.at[to, :, lanes(chunk)],
                    dst_ref=dst.at[me, :, lanes(chunk)],
                    send_sem=send_sem.at[chunk, i],
                    recv_sem=recv_sem.at[chunk, i],
                    device_id={"seq": to},
                    device_id_type=MESH,
                ).start()
            return carry

        lax.fori_loop(1, n, send, 0)

    def chunk_copies(chunk):
        return [
            pltpu.make_async_remote_copy(
                src_ref=src.at[pl.ds(0, n - 1), :, lanes(chunk)],
                dst_ref=dst.at[pl.ds(0, n - 1), :, lanes(chunk)],
                send_sem=send_sem.at[chunk, i],
                recv_sem=recv_sem.at[chunk, i],
                device_id={"seq": peer(1)},
                device_id_type=MESH,
            )
            for i, (src, dst) in enumerate(forward)
        ]

    def back_copies(chunk):
        return pltpu.make_async_remote_copy(
            src_ref=back.at[pl.ds(0, n - 1), :, lanes(chunk)],
            dst_ref=home.at[pl.ds(0, n - 1), :, lanes(chunk)],
            send_sem=back_send.at[chunk],
            recv_sem=back_recv.at[chunk],
            device_id={"seq": peer(1)},
            device_id_type=MESH,
        )

    lane = lax.broadcasted_iota(jnp.int32, (tokens, HD), 1)

    def keep(stats, head, high, total):
        stats[...] = jnp.where(
            lane == head, high, jnp.where(lane == head + HEADS, total, stats[...])
        )

    def row_chunk(chunk):
        for sub in range(CHUNK_HEADS):
            head = chunk * CHUNK_HEADS + sub
            at = pl.ds(head * HD, HD)
            out, high, total = attend(
                q_ref[:, :, at].reshape(tokens, HD),
                k_ref[:, :, at].reshape(tokens, HD),
                v_ref[:, :, at].reshape(tokens, HD),
                row_bias[...],
            )
            row_out[:, at] = out.astype(jnp.bfloat16)
            keep(row_stats, head, high, total)

    def col_chunk(chunk):
        for sub in range(CHUNK_HEADS):
            head = chunk * CHUNK_HEADS + sub
            at = pl.ds(head * HD, HD)
            out, high, total = attend(
                q_all[:, :, at].reshape(tokens, HD),
                k_all[:, :, at].reshape(tokens, HD),
                v_all[:, :, at].reshape(tokens, HD),
                col_bias[...],
            )
            back[:, :, at] = out.astype(jnp.bfloat16).reshape(n, cols, HD)
            keep(col_stats, head, high, total)

    row_stats[...] = jnp.zeros_like(row_stats)
    col_stats[...] = jnp.zeros_like(col_stats)

    for chunk in range(chunks):
        send_chunk(chunk)

    def row_step(chunk, carry):
        row_chunk(chunk)
        return carry

    lax.fori_loop(0, chunks, row_step, 0)

    for copy in own:
        copy.wait()

    def col_step(chunk, carry):
        for copy in chunk_copies(chunk):
            copy.wait_recv()
        col_chunk(chunk)

        def send_back(step, inner):
            to = peer(step)
            pltpu.make_async_remote_copy(
                src_ref=back.at[to, :, lanes(chunk)],
                dst_ref=home.at[me, :, lanes(chunk)],
                send_sem=back_send.at[chunk],
                recv_sem=back_recv.at[chunk],
                device_id={"seq": to},
                device_id_type=MESH,
            ).start()
            return inner

        lax.fori_loop(1, n, send_back, 0)
        return carry

    lax.fori_loop(0, chunks, col_step, 0)


    def send_stats(step, carry):
        to = peer(step)
        pltpu.make_async_remote_copy(
            src_ref=col_stats.at[pl.ds(pl.multiple_of(to * cols, cols), cols)],
            dst_ref=home_stats.at[pl.ds(pl.multiple_of(me * cols, cols), cols)],
            send_sem=stat_send,
            recv_sem=stat_recv,
            device_id={"seq": to},
            device_id_type=MESH,
        ).start()
        return carry

    lax.fori_loop(1, n, send_stats, 0)
    home[me] = back[me]
    mine = pl.ds(pl.multiple_of(me * cols, cols), cols)
    home_stats[mine, :] = col_stats[mine, :]

    stat_all = pltpu.make_async_remote_copy(
        src_ref=col_stats.at[pl.ds(0, tokens - cols)],
        dst_ref=home_stats.at[pl.ds(0, tokens - cols)],
        send_sem=stat_send,
        recv_sem=stat_recv,
        device_id={"seq": peer(1)},
        device_id_type=MESH,
    )
    for chunk in range(chunks):
        for copy in chunk_copies(chunk):
            copy.wait_send()
    stat_all.wait()

    row_high, col_high = row_stats[...], home_stats[...]
    highest = jnp.maximum(row_high, col_high)
    row_factor = jnp.exp2((row_high - highest) * POWER)
    col_factor = jnp.exp2((col_high - highest) * POWER)
    row_total = pltpu.roll(row_high, HD - HEADS, 1)
    col_total = pltpu.roll(col_high, HD - HEADS, 1)
    total = row_total * row_factor + col_total * col_factor
    total = jnp.where(lane < HEADS, total, 1.0)
    row_factor = row_factor / total
    col_factor = col_factor / total

    for chunk in range(chunks):
        back_copies(chunk).wait()
        for sub in range(CHUNK_HEADS):
            head = chunk * CHUNK_HEADS + sub
            at = pl.ds(head * HD, HD)
            merged = row_out[:, at].astype(jnp.float32) * row_factor[:, head : head + 1]
            col_part = home[:, :, at].reshape(tokens, HD).astype(jnp.float32)
            merged = merged + col_part * col_factor[:, head : head + 1]
            out_ref[:, :, at] = merged.astype(jnp.bfloat16).reshape(n, cols, HD)


def local(query_vectors, key_vectors, value_vectors):
    n = lax.axis_size("seq")
    _, columns, width = query_vectors.shape
    cols = columns // n
    split = (n, cols, width)
    chunks = HEADS // CHUNK_HEADS
    vmem = pl.BlockSpec(memory_space=pltpu.VMEM)
    block = pltpu.VMEM(split, jnp.bfloat16)
    stats = pltpu.VMEM((columns, HD), jnp.float32)
    bias = pltpu.VMEM((columns, columns), jnp.float32)
    dma = pltpu.SemaphoreType.DMA
    finished = pl.pallas_call(
        functools.partial(kernel, n, cols),
        out_shape=jax.ShapeDtypeStruct(split, jnp.bfloat16),
        in_specs=[vmem] * 3,
        out_specs=vmem,
        scratch_shapes=[block] * 5
        + [pltpu.VMEM((columns, width), jnp.bfloat16)]
        + [stats] * 3
        + [bias] * 2
        + [dma((chunks, 3)), dma((chunks, 3)), dma((chunks,)), dma((chunks,)), dma, dma, dma((3,))],
        compiler_params=pltpu.CompilerParams(
            collective_id=0, has_side_effects=True, vmem_limit_bytes=40 * 2**20
        ),
        cost_estimate=pl.CostEstimate(
            flops=8 * columns * columns * width,
            bytes_accessed=8 * columns * width,
            transcendentals=2 * HEADS * columns * columns,
        ),
        name="strided_attention",
    )(
        query_vectors.reshape(split),
        key_vectors.reshape(split),
        value_vectors.reshape(split),
    )
    return finished.reshape(query_vectors.shape)


def solution(mesh):
    spec = P(("grp", "seq"), None, None)
    return jax.shard_map(
        local, mesh=mesh, in_specs=(spec, spec, spec), out_specs=spec, check_vma=False
    )
```

time: 375 us -> 210 us (0.56)
  Pallas kernels: 0 us -> 204 us
  waiting for transfers between devices: 138 us -> 0 us
  local copies, waits for them, and re-layouts: 68.2 us -> 4.65 us
  blocking collectives: 59.7 us -> 0 us
  starting transfers between devices: 54.9 us -> 0 us
  other arithmetic: 38.6 us -> 0 us
  matrix products: 9.89 us -> 0 us
    pallas_call x0 -> x1, Pallas kernels: none -> 204 us  [local(): pl.pallas_call(functools.partial(kernel, n, cols), out_shape=jax.ShapeDty...]
    all_to_all x6 -> x0, waiting for transfers between devices: 138 us -> none  [the longest x1 41.4 us: local(): lax.all_to_all(row_out, 'seq', split_axis=1, concat_axis=0, tiled=True)]
    all_to_all x1 -> x0, blocking collectives: 59.7 us -> none  [local(): lax.all_to_all(finished, 'seq', split_axis=0, concat_axis=1, tiled=True)]
    all_to_all x6 -> x0, starting transfers between devices: 54.9 us -> none  [the longest x1 17 us: local(): lax.all_to_all(row_total, 'seq', split_axis=1, concat_axis=0, tiled=True)]
    unnamed x41 -> x7, local copies, waits for them, and re-layouts: 40.6 us -> 4.65 us
    unnamed x6 -> x0, other arithmetic: 31.8 us -> none
    all_to_all x5 -> x0, local copies, waits for them, and re-layouts: 20.6 us -> none  [the longest x1 7.25 us: local(): lax.all_to_all(key_vectors, 'seq', split_axis=1, concat_axis=0, tiled=True)]
    dot_general x4 -> x0, matrix products: 9.89 us -> none  [the longest x2 7.14 us: attend(): jnp.einsum(blend_form, weights.astype(jnp.bfloat16), value_heads, preferr...]
  transfers between devices with their start and end apart: 6 -> 0, of which waited for: 5 -> 0; matrix products, arithmetic and copies ran while one was open for 25% -> 0% of each run, Pallas kernels for 0% -> 0%
where the time goes in v1:
time: 210 us; the launch traced here: 209 us
  Pallas kernels  204 us (97%)
  local copies, waits for them, and re-layouts  4.65 us (2%)
    pallas_call x1, Pallas kernels, local(): pl.pallas_call(functools.partial(kernel, n, cols), out_shape=jax.ShapeDty...  204 us
    unnamed x7, local copies, waits for them, and re-layouts  4.65 us

profile of v1, /device:TPU:1, one launch (start us, length us, event | category | flops | bytes accessed | tf_op | source)
XLA Modules:
  0.0 208.6 jit_solution(10492049185539354018)
XLA Ops:
  0.0 0.0 copy-start
  0.0 1.2 copy-done
  1.2 0.0 copy-start.1
  1.2 1.2 copy-done.1
  2.5 0.0 copy-start.2
  2.5 1.2 copy-done.2
  3.7 203.9 %strided_attention.1 = bf16[32,8,2048]{2,1,0:T(8,128)(2,1)S(1)} custom-call(bf16[32,8,2048]{2,1,0:T(8,128)(2,1)S(1)} %bitcast.5, bf16[32,8,2048]{2,1,0:T(8,128)(2,1)S(1)} %bitcast.6, bf16[32,8,2048]{2,1,0:T(8,128)(2,1)S(1)} %bitcast.7), custom_call_target="tpu_custom_call" | custom-call | flops 1073741824 | bytes 4194304 | tf_op jit(solution)/shard_map/strided_attention/pallas_call | solution.py:248
  207.6 1.0 copy.5
Async XLA Ops:
  0.0 1.2 copy-start
  1.2 1.2 copy-start.1
  2.5 1.2 copy-start.2

commit v2 on v1

--- a/solution.py
+++ b/solution.py
@@ -30,9 +30,9 @@
 
 def kernel(
     n, cols,
-    q_ref, k_ref, v_ref, out_ref,
-    q_all, k_all, v_all, back, home, row_out, row_stats, col_stats, home_stats, row_bias, col_bias,
-    send_sem, recv_sem, back_send, back_recv, stat_send, stat_recv, own_sem,
+    q_hbm, k_hbm, v_hbm, out_ref,
+    q_ref, k_ref, v_ref, q_all, k_all, v_all, back, home, row_out, row_stats, col_stats, stats_out, stats_in, home_stats, row_bias, col_bias,
+    send_sem, recv_sem, back_send, back_recv, stat_send, stat_recv, own_sem, load_sem,
 ):
     me = lax.axis_index("seq")
     width = CHUNK_HEADS * HD
@@ -43,6 +43,10 @@
     def peer(step):
         return lax.rem(me + step, n)
 
+    def far_first(turn):
+        away = lax.div(turn + 1, 2)
+        return peer(n // 2 + away * (2 * lax.rem(turn, 2) - 1))
+
     barrier = pltpu.get_barrier_semaphore()
 
     def greet(step, carry):
@@ -53,12 +57,16 @@
 
     lax.fori_loop(1, n, greet, 0)
 
+    loads = [
+        pltpu.make_async_copy(src, dst, load_sem.at[i])
+        for i, (src, dst) in enumerate(((q_hbm, q_ref), (k_hbm, k_ref), (v_hbm, v_ref)))
+    ]
+    for copy in loads:
+        copy.start()
     own = [
         pltpu.make_async_copy(src.at[me], dst.at[me], own_sem.at[i])
         for i, (src, dst) in enumerate(forward)
     ]
-    for copy in own:
-        copy.start()
 
     index = lax.broadcasted_iota(jnp.int32, (tokens, tokens), 0)
     other = lax.broadcasted_iota(jnp.int32, (tokens, tokens), 1)
@@ -67,6 +75,12 @@
     before = lax.div(other, cols) < lax.div(index, cols)
     col_bias[...] = jnp.where(same & before, 0.0, FLOOR)
 
+    row_stats[...] = jnp.zeros_like(row_stats)
+    col_stats[...] = jnp.zeros_like(col_stats)
+    for load, copy in zip(loads, own):
+        load.wait()
+        copy.start()
+
     pl.semaphore_wait(barrier, n - 1)
 
     def lanes(chunk):
@@ -74,7 +88,7 @@
 
     def send_chunk(chunk):
         def send(step, carry):
-            to = peer(step)
+            to = far_first(step)
             for i, (src, dst) in enumerate(forward):
                 pltpu.make_async_remote_copy(
                     src_ref=src.at[to, :, lanes(chunk)],
@@ -86,7 +100,7 @@
                 ).start()
             return carry
 
-        lax.fori_loop(1, n, send, 0)
+        lax.fori_loop(0, n - 1, send, 0)
 
     def chunk_copies(chunk):
         return [
@@ -144,9 +158,6 @@
             back[:, :, at] = out.astype(jnp.bfloat16).reshape(n, cols, HD)
             keep(col_stats, head, high, total)
 
-    row_stats[...] = jnp.zeros_like(row_stats)
-    col_stats[...] = jnp.zeros_like(col_stats)
-
     for chunk in range(chunks):
         send_chunk(chunk)
 
@@ -165,7 +176,7 @@
         col_chunk(chunk)
 
         def send_back(step, inner):
-            to = peer(step)
+            to = far_first(step)
             pltpu.make_async_remote_copy(
                 src_ref=back.at[to, :, lanes(chunk)],
                 dst_ref=home.at[me, :, lanes(chunk)],
@@ -176,17 +187,28 @@
             ).start()
             return inner
 
-        lax.fori_loop(1, n, send_back, 0)
+        lax.fori_loop(0, n - 1, send_back, 0)
         return carry
 
     lax.fori_loop(0, chunks, col_step, 0)
 
 
+    wide = lax.broadcasted_iota(jnp.int32, (n, HD), 1)
+    highs = jnp.zeros((n, HD), jnp.float32)
+    totals = highs
+    for column in range(cols):
+        part = col_stats[pl.ds(column, n, stride=cols), :]
+        here = lax.div(wide, HEADS) == column
+        highs = jnp.where(here, pltpu.roll(part, column * HEADS, 1), highs)
+        totals = jnp.where(here, pltpu.roll(part, (column - 1) * HEADS % HD, 1), totals)
+    stats_out[:, 0, :] = highs
+    stats_out[:, 1, :] = totals
+
     def send_stats(step, carry):
-        to = peer(step)
+        to = far_first(step)
         pltpu.make_async_remote_copy(
-            src_ref=col_stats.at[pl.ds(pl.multiple_of(to * cols, cols), cols)],
-            dst_ref=home_stats.at[pl.ds(pl.multiple_of(me * cols, cols), cols)],
+            src_ref=stats_out.at[to],
+            dst_ref=stats_in.at[me],
             send_sem=stat_send,
             recv_sem=stat_recv,
             device_id={"seq": to},
@@ -194,14 +216,13 @@
         ).start()
         return carry
 
-    lax.fori_loop(1, n, send_stats, 0)
+    lax.fori_loop(0, n - 1, send_stats, 0)
     home[me] = back[me]
-    mine = pl.ds(pl.multiple_of(me * cols, cols), cols)
-    home_stats[mine, :] = col_stats[mine, :]
+    stats_in[me] = stats_out[me]
 
     stat_all = pltpu.make_async_remote_copy(
-        src_ref=col_stats.at[pl.ds(0, tokens - cols)],
-        dst_ref=home_stats.at[pl.ds(0, tokens - cols)],
+        src_ref=stats_out.at[pl.ds(0, n - 1)],
+        dst_ref=stats_in.at[pl.ds(0, n - 1)],
         send_sem=stat_send,
         recv_sem=stat_recv,
         device_id={"seq": peer(1)},
@@ -212,6 +233,13 @@
             copy.wait_send()
     stat_all.wait()
 
+    highs, totals = stats_in[:, 0, :], stats_in[:, 1, :]
+    for column in range(cols):
+        back_high = pltpu.roll(highs, -column * HEADS % HD, 1)
+        back_total = pltpu.roll(totals, (1 - column) * HEADS % HD, 1)
+        home_stats[pl.ds(column, n, stride=cols), :] = jnp.where(
+            wide < HEADS, back_high, back_total
+        )
     row_high, col_high = row_stats[...], home_stats[...]
     highest = jnp.maximum(row_high, col_high)
     row_factor = jnp.exp2((row_high - highest) * POWER)
@@ -248,15 +276,17 @@
     finished = pl.pallas_call(
         functools.partial(kernel, n, cols),
         out_shape=jax.ShapeDtypeStruct(split, jnp.bfloat16),
-        in_specs=[vmem] * 3,
+        in_specs=[pl.BlockSpec(memory_space=pl.ANY)] * 3,
         out_specs=vmem,
-        scratch_shapes=[block] * 5
+        scratch_shapes=[block] * 8
         + [pltpu.VMEM((columns, width), jnp.bfloat16)]
-        + [stats] * 3
+        + [stats] * 2
+        + [pltpu.VMEM((n, 2, HD), jnp.float32)] * 2
+        + [stats]
         + [bias] * 2
-        + [dma((chunks, 3)), dma((chunks, 3)), dma((chunks,)), dma((chunks,)), dma, dma, dma((3,))],
+        + [dma((chunks, 3)), dma((chunks, 3)), dma((chunks,)), dma((chunks,)), dma, dma, dma((3,)), dma((3,))],
         compiler_params=pltpu.CompilerParams(
-            collective_id=0, has_side_effects=True, vmem_limit_bytes=40 * 2**20
+            collective_id=0, has_side_effects=True, vmem_limit_bytes=56 * 2**20
         ),
         cost_estimate=pl.CostEstimate(
             flops=8 * columns * columns * width,

time: 210 us -> 206 us (0.981)
  local copies, waits for them, and re-layouts: 4.65 us -> 2.3 us
    unnamed x7 -> x1, local copies, waits for them, and re-layouts: 4.65 us -> 2.3 us
where the time goes in v2:
time: 206 us
  Pallas kernels  204 us (99%)
  local copies, waits for them, and re-layouts  2.3 us (1%)
    pallas_call x1, Pallas kernels, local(): pl.pallas_call(functools.partial(kernel, n, cols), out_shape=jax.ShapeDty...  204 us

profile of v2, /device:TPU:1, one launch (start us, length us, event | category | flops | bytes accessed | tf_op | source)
XLA Modules:
  0.0 206.1 jit_solution(5700042814991116244)
XLA Ops:
  0.0 203.8 %strided_attention.1 = bf16[32,8,2048]{2,1,0:T(8,128)(2,1)} custom-call(bf16[32,8,2048]{2,1,0:T(8,128)(2,1)} %bitcast.5, bf16[32,8,2048]{2,1,0:T(8,128)(2,1)} %bitcast.6, bf16[32,8,2048]{2,1,0:T(8,128)(2,1)} %bitcast.7), custom_call_target="tpu_custom_call" | custom-call | flops 1073741824 | bytes 4194304 | tf_op jit(solution)/shard_map/strided_attention/pallas_call | solution.py:276
  203.8 2.3 %copy.5 = bf16[1,256,2048]{2,1,0:T(8,128)(2,1)} copy(bf16[1,256,2048]{2,1,0:T(8,128)(2,1)} %bitcast.4) | data formatting | bytes 2097152

commit v3 on v0

v3 whole, which is shorter than its diff:
```python
import functools
import math

import jax
import jax.numpy as jnp
from jax import lax
from jax.experimental import pallas as pl
from jax.experimental.pallas import tpu as pltpu
from jax.sharding import PartitionSpec as P

HEADS = 16
HD = 128
FLOOR = -1e30
POWER = math.log2(math.e) / math.sqrt(HD)
CHUNK_HEADS = 8
CHUNKS = HEADS // CHUNK_HEADS
WIDTH = CHUNK_HEADS * HD
MESH = pl.DeviceIdType.MESH

ROLES = (
    (1, 0, 0x701F, 0xFE06), (15, 16, 0x1FFF, 0xFFF0), (27, 8, 0x03FF, 0xFFFE),
    (21, 24, 0x3FFF, 0xFFE0), (19, 4, 0x41FF, 0xFFFE), (17, 20, 0x7F00, 0xFE00),
    (30, 12, 0x0FFF, 0xFFFC), (29, 28, 0x701F, 0xFFFE), (11, 2, 0x7FFF, 0xFFFE),
    (2, 18, 0x1FE0, 0xFFC0), (5, 10, 0x07FF, 0xFFF8), (23, 26, 0x701F, 0xFF06),
    (22, 6, 0x03FF, 0xFFFE), (8, 22, 0x7FFF, 0xFFE0), (13, 14, 0x1FFF, 0xFFF0),
    (25, 30, 0x607F, 0xFFFE), (0, 1, 0x701F, 0xFE02), (24, 17, 0x0FF0, 0xFFE0),
    (28, 9, 0x03FF, 0xFFFE), (18, 25, 0x780F, 0xFFC0), (9, 5, 0x41FF, 0xFFFC),
    (25, 21, 0x1F80, 0xFF00), (12, 13, 0x07FF, 0xFFF0), (31, 29, 0x603F, 0xFFFE),
    (10, 3, 0x0007, 0x000E), (0, 19, 0x0FE0, 0xFFC0), (6, 11, 0x07FF, 0xFFF8),
    (22, 27, 0x7C00, 0xF800), (3, 7, 0x03FF, 0xFFFC), (20, 23, 0x0FFF, 0xFFE0),
    (14, 15, 0x1FFF, 0xFFF0), (24, 31, 0x700F, 0xFF06), (2, 1, 0x601F, 0xFE06),
    (18, 17, 0x07F0, 0xFFE0), (26, 9, 0x00FF, 0x01F8), (27, 25, 0x7C00, 0xF800),
    (17, 5, 0x00FF, 0xFFFE), (31, 21, 0x1FC0, 0xFE00), (16, 13, 0x07FF, 0xFFF0),
    (3, 29, 0x7C00, 0xF800), (12, 3, 0x0007, 0x000E), (1, 19, 0x0FE0, 0xFFC0),
    (5, 27, 0x7800, 0xF000), (0, 7, 0x001F, 0x01FC), (9, 23, 0x3E00, 0xFC00),
    (26, 31, 0x603F, 0xFE06), (7, 0, 0x0007, 0x000E), (23, 16, 0x0FE0, 0xFF00),
    (4, 8, 0x07FF, 0xFFF8), (28, 24, 0x7C00, 0xF800), (18, 4, 0x000F, 0x003E),
    (26, 20, 0x1FC0, 0xFE00), (29, 12, 0x0060, 0x00C0), (7, 28, 0x603F, 0xFFF0),
    (15, 2, 0x0007, 0x000E), (7, 18, 0x1FC0, 0xFF80), (10, 10, 0x07FF, 0xFFF0),
    (6, 26, 0x7800, 0xF000), (23, 6, 0x007F, 0x00F8), (19, 22, 0x3E00, 0xF800),
    (31, 14, 0x00C0, 0x0180), (4, 30, 0x7800, 0xF000), (4, 0, 0x0003, 0x0006),
    (20, 4, 0x000F, 0x001E), (19, 20, 0x0200, 0x0400), (30, 28, 0x0001, 0x0002),
    (8, 2, 0x0001, 0x0002), (29, 18, 0x0FE0, 0xFF00), (16, 26, 0x7800, 0xF000),
    (2, 6, 0x001F, 0x01F8), (13, 30, 0x6000, 0xC000), (6, 1, 0x0003, 0x0006),
    (8, 5, 0x000F, 0x001C), (12, 29, 0x7800, 0xF000), (13, 3, 0x0007, 0x000E),
    (10, 27, 0x7800, 0xF000), (1, 7, 0x001F, 0x01F8), (14, 31, 0x6000, 0xC000),
    (3, 1, 0x0001, 0x0002), (16, 5, 0x0007, 0x000E), (20, 29, 0x7000, 0xE000),
    (14, 3, 0x0007, 0x000E), (30, 27, 0x7000, 0xE000), (24, 7, 0x000F, 0x00F8),
    (21, 31, 0x4000, 0x8000), (5, 0, 0x0003, 0x0006), (21, 4, 0x000F, 0x001E),
    (9, 2, 0x0001, 0x0002), (15, 30, 0x6000, 0xC000),
)


def slots_of(n):
    taken = [0] * n
    seen = {}
    out = []
    for group, device, key_mask, query_mask in ROLES:
        before = seen.get(group, 0)
        seen[group] = before | query_mask
        out.append((group, device, taken[device], key_mask, query_mask, before & query_mask))
        taken[device] += 1
    return out, taken


def attend(queries, keys, values, bias, strict):
    scores = lax.dot_general(
        queries, keys, (((1,), (1,)), ((), ())), preferred_element_type=jnp.float32
    )
    scores = jnp.where(bias == 0.0, scores, FLOOR) if strict else scores + bias
    high = jnp.max(scores, axis=1, keepdims=True)
    weights = jnp.exp2((scores - high) * POWER)
    total = jnp.sum(weights, axis=1, keepdims=True)
    out = jnp.dot(weights.astype(jnp.bfloat16), values, preferred_element_type=jnp.float32)
    return out, high, total


def kernel(
    n, cols, slots,
    q_hbm, k_hbm, v_hbm, out_ref,
    q_ref, k_ref, v_ref, q_all, k_all, v_all, back, home, k_pair, v_pair, row_out,
    row_stats, pair_stats, col_stats, stats_out, stats_in, home_stats, row_bias, col_bias,
    load_sem, send_sem, recv_sem, back_send, back_recv, stat_send, stat_recv, pair_send, pair_recv,
):
    me = lax.axis_index("seq")
    layer, side = lax.div(me, 2), lax.rem(me, 2)
    tokens = n * cols
    layers = n // 2
    roles, taken = slots_of(n)
    sources = ((q_ref, q_all), (k_ref, k_all), (v_ref, v_all))

    def pick(values, index):
        out = index * 0
        for i, value in enumerate(values):
            if value:
                out = jnp.where(index == i, value, out)
        return out

    def when_count(values, index, act):
        chosen = pick(values, index)
        for value in sorted(set(values)):
            if value:
                pl.when(chosen == value)(functools.partial(act, value))

    def layer_bit(mask):
        return pick([mask >> i & 1 for i in range(layers)], layer)

    def table(slot, field, default=0):
        values = [default] * n
        for role in roles:
            if role[2] == slot:
                values[role[1]] = role[field]
        return values

    def lanes(chunk):
        return pl.ds(chunk * WIDTH, WIDTH)

    v_all[...] = jnp.zeros_like(v_all)
    home[...] = jnp.zeros_like(home)
    empty = lax.broadcasted_iota(jnp.int32, (n, 2, HD), 1)
    for part in range(2):
        stats_in[part] = jnp.where(empty == 0, FLOOR, 0.0)

    barrier = pltpu.get_barrier_semaphore()

    def greet(step, carry):
        pl.semaphore_signal(
            barrier, inc=1, device_id={"seq": lax.rem(me + step, n)}, device_id_type=MESH
        )
        return carry

    lax.fori_loop(1, n, greet, 0)

    loads = [
        pltpu.make_async_copy(src, dst, load_sem.at[i])
        for i, (src, dst) in enumerate(((q_hbm, q_ref), (k_hbm, k_ref), (v_hbm, v_ref)))
    ]
    for copy in loads:
        copy.start()

    index = lax.broadcasted_iota(jnp.int32, (tokens, tokens), 0)
    other = lax.broadcasted_iota(jnp.int32, (tokens, tokens), 1)
    row_bias[...] = jnp.where(other <= index, 0.0, FLOOR)
    index_layer = lax.div(index, 2 * cols)
    other_layer = lax.div(other, 2 * cols)
    below = (lax.rem(index, cols) == lax.rem(other, cols)) & (other_layer < index_layer)
    slot_group, slot_queries, slot_second = [], [], []
    for slot in range(slots):
        key_bits = pick(table(slot, 3), me)
        query_bits = pick(table(slot, 4), me)
        slot_group.append(pick(table(slot, 0), me))
        slot_queries.append(query_bits)
        slot_second.append(pick(table(slot, 5), me))
        allowed = (jnp.right_shift(query_bits, index_layer) & 1) * (
            jnp.right_shift(key_bits, other_layer) & 1
        )
        col_bias[slot] = jnp.where(below & (allowed == 1), 0.0, FLOOR)
    row_stats[...] = jnp.zeros_like(row_stats)
    pair_stats[...] = jnp.zeros_like(pair_stats)
    col_stats[...] = jnp.zeros_like(col_stats)
    for copy in loads:
        copy.wait()

    pl.semaphore_wait(barrier, n - 1)

    pairs = ((k_ref, k_pair), (v_ref, v_pair))
    pair_copies = [
        pltpu.make_async_remote_copy(
            src_ref=src, dst_ref=dst, send_sem=pair_send.at[i], recv_sem=pair_recv.at[i],
            device_id={"seq": lax.rem(me + 1, n)}, device_id_type=MESH,
        )
        for i, (src, dst) in enumerate(pairs)
    ]
    own_copies = [
        pltpu.make_async_copy(src, dst, pair_recv.at[i]) for i, (src, dst) in enumerate(pairs)
    ]

    def send_forward(chunk, carry):
        for group, device, slot, key_mask, query_mask, _ in roles:
            for wanted, arrays in ((key_mask, (1, 2)), (query_mask, (0,))):

                def go(group=group, device=device, slot=slot, arrays=arrays):
                    for i in arrays:
                        src, dst = sources[i]
                        pltpu.make_async_remote_copy(
                            src_ref=src.at[group, :, lanes(chunk)],
                            dst_ref=dst.at[slot, me, :, lanes(chunk)],
                            send_sem=send_sem.at[chunk, i],
                            recv_sem=recv_sem.at[slot, chunk, i],
                            device_id={"seq": me * 0 + device},
                            device_id_type=MESH,
                        ).start()

                pl.when((layer_bit(wanted) == 1) & (me != device))(go)
        return carry

    def own_forward(chunk, carry):
        for slot in range(slots):
            for field, arrays in ((3, (1, 2)), (4, (0,))):
                wanted = [
                    1 if mask >> (i // 2) & 1 else 0 for i, mask in enumerate(table(slot, field))
                ]

                def go(slot=slot, arrays=arrays):
                    for i in arrays:
                        src, dst = sources[i]
                        pltpu.make_async_copy(
                            src.at[slot_group[slot], :, lanes(chunk)],
                            dst.at[slot, me, :, lanes(chunk)],
                            recv_sem.at[slot, chunk, i],
                        ).start()

                pl.when(pick(wanted, me) == 1)(go)
        return carry

    def wait_forward(slot, chunk):
        for i, field in ((0, 4), (1, 3), (2, 3)):
            src, dst = sources[i]
            counts = [2 * mask.bit_count() for mask in table(slot, field)]

            def act(count, i=i, dst=dst):
                pltpu.make_async_copy(
                    dst.at[slot, pl.ds(0, count), :, lanes(chunk)],
                    dst.at[slot, pl.ds(0, count), :, lanes(chunk)],
                    recv_sem.at[slot, chunk, i],
                ).wait()

            when_count(counts, me, act)

    lane = lax.broadcasted_iota(jnp.int32, (tokens, HD), 1)

    def kept(stats, head, high, total):
        return jnp.where(lane == head, high, jnp.where(lane == head + HEADS, total, stats))

    def row_step(turn, carry):
        for sub in range(2):
            head = turn * 2 + sub
            at = pl.ds(pl.multiple_of(head * HD, HD), HD)
            out, high, total = attend(
                q_ref[:, :, at].reshape(tokens, HD),
                k_ref[:, :, at].reshape(tokens, HD),
                v_ref[:, :, at].reshape(tokens, HD),
                row_bias[...],
                False,
            )
            row_out[:, at] = out.astype(jnp.bfloat16)
            row_stats[...] = kept(row_stats[...], head, high, total)
        return carry

    def col_heads(slot, chunk):
        def step(turn, carry):
            for sub in range(2):
                head = chunk * CHUNK_HEADS + turn * 2 + sub
                at = pl.ds(pl.multiple_of(head * HD, HD), HD)
                out, high, total = attend(
                    q_all[slot, :, :, at].reshape(tokens, HD),
                    k_all[slot, :, :, at].reshape(tokens, HD),
                    v_all[slot, :, :, at].reshape(tokens, HD),
                    col_bias[slot],
                    True,
                )
                back[slot, :, :, at] = out.astype(jnp.bfloat16).reshape(n, cols, HD)
                col_stats[slot] = kept(col_stats[slot], head, high, total)
            return carry

        lax.fori_loop(0, CHUNK_HEADS // 2, step, 0)

    def each_row(slot, act):
        def step(turn, carry):
            row = lax.rem(me + turn, n)
            wanted = jnp.right_shift(slot_queries[slot], lax.div(row, 2)) & 1
            part = jnp.right_shift(slot_second[slot], lax.div(row, 2)) & 1
            pl.when((wanted == 1) & (turn > 0))(lambda: act(row, part, True))
            pl.when((wanted == 1) & (turn == 0))(lambda: act(row, part, False))
            return carry

        lax.fori_loop(0, n, step, 0)

    def send_back(slot, chunk):
        def act(row, part, far):
            src = back.at[slot, row, :, lanes(chunk)]
            dst = home.at[part, slot_group[slot], :, lanes(chunk)]
            if far:
                pltpu.make_async_remote_copy(
                    src_ref=src, dst_ref=dst,
                    send_sem=back_send.at[slot, chunk], recv_sem=back_recv.at[part, chunk],
                    device_id={"seq": row}, device_id_type=MESH,
                ).start()
            else:
                pltpu.make_async_copy(src, dst, back_recv.at[part, chunk]).start()

        each_row(slot, act)

    wide = lax.broadcasted_iota(jnp.int32, (n, HD), 1)

    def send_stats(slot):
        highs = jnp.zeros((n, HD), jnp.float32)
        totals = highs
        for column in range(cols):
            part = col_stats[slot, pl.ds(column, n, stride=cols), :]
            here = lax.div(wide, HEADS) == column
            highs = jnp.where(here, pltpu.roll(part, column * HEADS, 1), highs)
            totals = jnp.where(here, pltpu.roll(part, (column - 1) * HEADS % HD, 1), totals)
        stats_out[slot, :, 0, :] = highs
        stats_out[slot, :, 1, :] = totals

        def act(row, part, far):
            src = stats_out.at[slot, row]
            dst = stats_in.at[part, slot_group[slot]]
            if far:
                pltpu.make_async_remote_copy(
                    src_ref=src, dst_ref=dst,
                    send_sem=stat_send.at[slot], recv_sem=stat_recv.at[part],
                    device_id={"seq": row}, device_id_type=MESH,
                ).start()
            else:
                pltpu.make_async_copy(src, dst, stat_recv.at[part]).start()

        each_row(slot, act)

    lax.fori_loop(0, CHUNKS, send_forward, 0)
    lax.fori_loop(0, CHUNKS, own_forward, 0)

    @pl.when(side == 0)
    def _():
        for copy in pair_copies + own_copies:
            copy.start()

    lax.fori_loop(0, HEADS // 2, row_step, 0)

    for chunk in range(CHUNKS):
        for slot in range(slots):
            present = pick([1 if taken[i] > slot else 0 for i in range(n)], me) == 1

            @pl.when(present)
            def _(slot=slot, chunk=chunk):
                wait_forward(slot, chunk)
                col_heads(slot, chunk)
                send_back(slot, chunk)
                if chunk == CHUNKS - 1:
                    send_stats(slot)

    for i, (src, dst) in enumerate(pairs):
        pltpu.make_async_copy(src, dst, pair_recv.at[i]).wait()

    def pair_step(head, carry):
        at = pl.ds(pl.multiple_of(head * HD, HD), HD)
        product = q_ref[:, :, at].reshape(tokens, HD).astype(jnp.float32) * k_pair[
            :, :, at
        ].reshape(tokens, HD).astype(jnp.float32)
        high = jnp.sum(product, axis=1, keepdims=True)
        pair_stats[...] = kept(pair_stats[...], head, high, 1.0)
        return carry

    lax.fori_loop(0, HEADS, pair_step, 0)

    parts = [[0] * layers for _ in range(2)]
    for _, _, _, _, query_mask, second in roles:
        for i in range(layers):
            if query_mask >> i & 1:
                parts[second >> i & 1][i] += 1

    for part in range(2):

        def act(count, part=part):
            pltpu.make_async_copy(
                stats_in.at[part, pl.ds(0, count)], stats_in.at[part, pl.ds(0, count)],
                stat_recv.at[part],
            ).wait()

        when_count(parts[part], layer, act)

    def merged_stats(part):
        highs, totals = stats_in[part, :, 0, :], stats_in[part, :, 1, :]
        for column in range(cols):
            back_high = pltpu.roll(highs, -column * HEADS % HD, 1)
            back_total = pltpu.roll(totals, (1 - column) * HEADS % HD, 1)
            home_stats[pl.ds(column, n, stride=cols), :] = jnp.where(
                wide < HEADS, back_high, back_total
            )
        return home_stats[...]

    offset = jnp.where(side == 1, 0.0, FLOOR)
    pair_high = jnp.where(lane < HEADS, pair_stats[...] + offset, pair_stats[...])
    terms = [row_stats[...], merged_stats(0), merged_stats(1), pair_high]
    highest = functools.reduce(jnp.maximum, terms)
    factors = [jnp.exp2((term - highest) * POWER) for term in terms]
    total = sum(pltpu.roll(term, HD - HEADS, 1) * f for term, f in zip(terms, factors))
    total = jnp.where(lane < HEADS, total, 1.0)
    factors = [f / total for f in factors]

    for chunk in range(CHUNKS):
        for part in range(2):

            def act(count, part=part, chunk=chunk):
                pltpu.make_async_copy(
                    home.at[part, pl.ds(0, count), :, lanes(chunk)],
                    home.at[part, pl.ds(0, count), :, lanes(chunk)],
                    back_recv.at[part, chunk],
                ).wait()

            when_count(parts[part], layer, act)
        for sub in range(CHUNK_HEADS):
            head = chunk * CHUNK_HEADS + sub
            at = pl.ds(head * HD, HD)
            blocks = (
                row_out[:, at],
                home[0, :, :, at].reshape(tokens, HD),
                home[1, :, :, at].reshape(tokens, HD),
                v_pair[:, :, at].reshape(tokens, HD),
            )
            merged = sum(
                block.astype(jnp.float32) * f[:, head : head + 1]
                for block, f in zip(blocks, factors)
            )
            out_ref[:, :, at] = merged.astype(jnp.bfloat16).reshape(n, cols, HD)

    sent_keys = [0] * n
    sent_queries = [0] * n
    for _, device, _, key_mask, query_mask, _ in roles:
        for i in range(n):
            if i != device:
                sent_keys[i] += key_mask >> (i // 2) & 1
                sent_queries[i] += query_mask >> (i // 2) & 1
    for chunk in range(CHUNKS):
        for i, counts in ((0, sent_queries), (1, sent_keys), (2, sent_keys)):
            src, dst = sources[i]

            def act(count, i=i, dst=dst, chunk=chunk):
                whole, rest = count // n, count % n
                for size in [n] * whole + [rest] * (rest > 0):
                    pltpu.make_async_remote_copy(
                        src_ref=dst.at[0, pl.ds(0, size), :, lanes(chunk)],
                        dst_ref=dst.at[0, pl.ds(0, size), :, lanes(chunk)],
                        send_sem=send_sem.at[chunk, i], recv_sem=recv_sem.at[0, chunk, i],
                        device_id={"seq": lax.rem(me + 1, n)}, device_id_type=MESH,
                    ).wait_send()

            when_count(counts, me, act)
    for slot in range(slots):
        counts = [
            2 * mask.bit_count() - (mask >> (i // 2) & 1)
            for i, mask in enumerate(table(slot, 4))
        ]

        def act(count, slot=slot):
            for chunk in range(CHUNKS):
                pltpu.make_async_remote_copy(
                    src_ref=back.at[slot, pl.ds(0, count), :, lanes(chunk)],
                    dst_ref=back.at[slot, pl.ds(0, count), :, lanes(chunk)],
                    send_sem=back_send.at[slot, chunk], recv_sem=back_recv.at[0, chunk],
                    device_id={"seq": lax.rem(me + 1, n)}, device_id_type=MESH,
                ).wait_send()
            pltpu.make_async_remote_copy(
                src_ref=stats_out.at[slot, pl.ds(0, count)],
                dst_ref=stats_out.at[slot, pl.ds(0, count)],
                send_sem=stat_send.at[slot], recv_sem=stat_recv.at[0],
                device_id={"seq": lax.rem(me + 1, n)}, device_id_type=MESH,
            ).wait_send()

        when_count(counts, me, act)

    @pl.when(side == 0)
    def _():
        for copy in pair_copies:
            copy.wait_send()


def local(query_vectors, key_vectors, value_vectors):
    n = lax.axis_size("seq")
    _, columns, width = query_vectors.shape
    cols = columns // n
    split = (n, cols, width)
    slots = max(slots_of(n)[1])
    block = pltpu.VMEM(split, jnp.bfloat16)
    blocks = pltpu.VMEM((slots,) + split, jnp.bfloat16)
    stats = pltpu.VMEM((columns, HD), jnp.float32)
    dma = pltpu.SemaphoreType.DMA
    finished = pl.pallas_call(
        functools.partial(kernel, n, cols, slots),
        out_shape=jax.ShapeDtypeStruct(split, jnp.bfloat16),
        in_specs=[pl.BlockSpec(memory_space=pl.ANY)] * 3,
        out_specs=pl.BlockSpec(memory_space=pltpu.VMEM),
        scratch_shapes=[block] * 3
        + [blocks] * 4
        + [pltpu.VMEM((2,) + split, jnp.bfloat16)]
        + [block] * 2
        + [pltpu.VMEM((columns, width), jnp.bfloat16)]
        + [stats] * 2
        + [pltpu.VMEM((slots, columns, HD), jnp.float32)]
        + [pltpu.VMEM((slots, n, 2, HD), jnp.float32), pltpu.VMEM((2, n, 2, HD), jnp.float32)]
        + [stats]
        + [pltpu.VMEM((columns, columns), jnp.float32)]
        + [pltpu.VMEM((slots, columns, columns), jnp.float32)]
        + [dma((3,)), dma((CHUNKS, 3)), dma((slots, CHUNKS, 3))]
        + [dma((slots, CHUNKS)), dma((2, CHUNKS)), dma((slots,)), dma((2,)), dma((2,)), dma((2,))],
        compiler_params=pltpu.CompilerParams(
            collective_id=0, has_side_effects=True, vmem_limit_bytes=56 * 2**20
        ),
        cost_estimate=pl.CostEstimate(
            flops=16 * columns * columns * width,
            bytes_accessed=8 * columns * width,
            transcendentals=4 * HEADS * columns * columns,
        ),
        name="strided_attention",
    )(
        query_vectors.reshape(split),
        key_vectors.reshape(split),
        value_vectors.reshape(split),
    )
    return finished.reshape(query_vectors.shape)


def solution(mesh):
    spec = P(("grp", "seq"), None, None)
    return jax.shard_map(
        local, mesh=mesh, in_specs=(spec, spec, spec), out_specs=spec, check_vma=False
    )
```

time: 375 us -> 191 us (0.51)
  the two profiles are of different devices: /device:TPU:1 before, /device:TPU:386 now
where the time goes in v3:
time: 191 us; the launch traced here: 190 us
  Pallas kernels  188 us (98%)
  local copies, waits for them, and re-layouts  2.3 us (1%)
    pallas_call x1, Pallas kernels, local(): pl.pallas_call(functools.partial(kernel, n, cols, slots), out_shape=jax.S...  188 us

profile of v3, /device:TPU:386, one launch (start us, length us, event | category | flops | bytes accessed | tf_op | source)
XLA Modules:
  0.0 190.5 jit_solution(15201895578871398606)
XLA Ops:
  0.0 188.2 %strided_attention.1 = bf16[32,8,2048]{2,1,0:T(8,128)(2,1)} custom-call(bf16[32,8,2048]{2,1,0:T(8,128)(2,1)} %bitcast.5, bf16[32,8,2048]{2,1,0:T(8,128)(2,1)} %bitcast.6, bf16[32,8,2048]{2,1,0:T(8,128)(2,1)} %bitcast.7), custom_call_target="tpu_custom_call" | custom-call | flops 2147483648 | bytes 4194304 | tf_op jit(solution)/shard_map/strided_attention/pallas_call | solution.py:479
  188.2 2.3 %copy.5 = bf16[1,256,2048]{2,1,0:T(8,128)(2,1)} copy(bf16[1,256,2048]{2,1,0:T(8,128)(2,1)} %bitcast.4) | data formatting | bytes 2097152

commit v4 on v3

--- a/solution.py
+++ b/solution.py
@@ -12,42 +12,43 @@
 HD = 128
 FLOOR = -1e30
 POWER = math.log2(math.e) / math.sqrt(HD)
-CHUNK_HEADS = 8
+CHUNK_HEADS = 4
 CHUNKS = HEADS // CHUNK_HEADS
 WIDTH = CHUNK_HEADS * HD
 MESH = pl.DeviceIdType.MESH
 
 ROLES = (
-    (1, 0, 0x701F, 0xFE06), (15, 16, 0x1FFF, 0xFFF0), (27, 8, 0x03FF, 0xFFFE),
-    (21, 24, 0x3FFF, 0xFFE0), (19, 4, 0x41FF, 0xFFFE), (17, 20, 0x7F00, 0xFE00),
-    (30, 12, 0x0FFF, 0xFFFC), (29, 28, 0x701F, 0xFFFE), (11, 2, 0x7FFF, 0xFFFE),
-    (2, 18, 0x1FE0, 0xFFC0), (5, 10, 0x07FF, 0xFFF8), (23, 26, 0x701F, 0xFF06),
-    (22, 6, 0x03FF, 0xFFFE), (8, 22, 0x7FFF, 0xFFE0), (13, 14, 0x1FFF, 0xFFF0),
-    (25, 30, 0x607F, 0xFFFE), (0, 1, 0x701F, 0xFE02), (24, 17, 0x0FF0, 0xFFE0),
-    (28, 9, 0x03FF, 0xFFFE), (18, 25, 0x780F, 0xFFC0), (9, 5, 0x41FF, 0xFFFC),
-    (25, 21, 0x1F80, 0xFF00), (12, 13, 0x07FF, 0xFFF0), (31, 29, 0x603F, 0xFFFE),
-    (10, 3, 0x0007, 0x000E), (0, 19, 0x0FE0, 0xFFC0), (6, 11, 0x07FF, 0xFFF8),
-    (22, 27, 0x7C00, 0xF800), (3, 7, 0x03FF, 0xFFFC), (20, 23, 0x0FFF, 0xFFE0),
-    (14, 15, 0x1FFF, 0xFFF0), (24, 31, 0x700F, 0xFF06), (2, 1, 0x601F, 0xFE06),
-    (18, 17, 0x07F0, 0xFFE0), (26, 9, 0x00FF, 0x01F8), (27, 25, 0x7C00, 0xF800),
-    (17, 5, 0x00FF, 0xFFFE), (31, 21, 0x1FC0, 0xFE00), (16, 13, 0x07FF, 0xFFF0),
-    (3, 29, 0x7C00, 0xF800), (12, 3, 0x0007, 0x000E), (1, 19, 0x0FE0, 0xFFC0),
-    (5, 27, 0x7800, 0xF000), (0, 7, 0x001F, 0x01FC), (9, 23, 0x3E00, 0xFC00),
-    (26, 31, 0x603F, 0xFE06), (7, 0, 0x0007, 0x000E), (23, 16, 0x0FE0, 0xFF00),
-    (4, 8, 0x07FF, 0xFFF8), (28, 24, 0x7C00, 0xF800), (18, 4, 0x000F, 0x003E),
-    (26, 20, 0x1FC0, 0xFE00), (29, 12, 0x0060, 0x00C0), (7, 28, 0x603F, 0xFFF0),
-    (15, 2, 0x0007, 0x000E), (7, 18, 0x1FC0, 0xFF80), (10, 10, 0x07FF, 0xFFF0),
-    (6, 26, 0x7800, 0xF000), (23, 6, 0x007F, 0x00F8), (19, 22, 0x3E00, 0xF800),
-    (31, 14, 0x00C0, 0x0180), (4, 30, 0x7800, 0xF000), (4, 0, 0x0003, 0x0006),
-    (20, 4, 0x000F, 0x001E), (19, 20, 0x0200, 0x0400), (30, 28, 0x0001, 0x0002),
-    (8, 2, 0x0001, 0x0002), (29, 18, 0x0FE0, 0xFF00), (16, 26, 0x7800, 0xF000),
-    (2, 6, 0x001F, 0x01F8), (13, 30, 0x6000, 0xC000), (6, 1, 0x0003, 0x0006),
-    (8, 5, 0x000F, 0x001C), (12, 29, 0x7800, 0xF000), (13, 3, 0x0007, 0x000E),
-    (10, 27, 0x7800, 0xF000), (1, 7, 0x001F, 0x01F8), (14, 31, 0x6000, 0xC000),
-    (3, 1, 0x0001, 0x0002), (16, 5, 0x0007, 0x000E), (20, 29, 0x7000, 0xE000),
-    (14, 3, 0x0007, 0x000E), (30, 27, 0x7000, 0xE000), (24, 7, 0x000F, 0x00F8),
-    (21, 31, 0x4000, 0x8000), (5, 0, 0x0003, 0x0006), (21, 4, 0x000F, 0x001E),
-    (9, 2, 0x0001, 0x0002), (15, 30, 0x6000, 0xC000),
+    (4, 0, 0x703F, 0xFE06), (22, 16, 0x07F0, 0xFFC0), (5, 8, 0x00FF, 0x01F8),
+    (22, 24, 0x780F, 0xFFC0), (8, 4, 0x41FF, 0xFFFC), (2, 20, 0x1FC0, 0xFE00),
+    (14, 12, 0x07FF, 0xFFF0), (24, 28, 0x781F, 0xFF82), (17, 2, 0x41FF, 0xFFFE),
+    (28, 18, 0x0FE0, 0xFFC0), (6, 10, 0x07FF, 0xFFFC), (19, 26, 0x7C00, 0xF800),
+    (10, 6, 0x03FF, 0xFFF8), (7, 22, 0x7FFF, 0xFFF8), (16, 14, 0x1FFF, 0xFFF0),
+    (29, 30, 0x603F, 0xFE06), (1, 1, 0x603F, 0xFE06), (23, 17, 0x0FFF, 0xFFF0),
+    (18, 9, 0x03FF, 0xFFF0), (21, 25, 0x7FFF, 0xFFC0), (9, 5, 0x41FF, 0xFFFC),
+    (1, 21, 0x1FC0, 0xFE00), (12, 13, 0x07FF, 0xFFF0), (27, 29, 0x701F, 0xFF86),
+    (13, 3, 0x0007, 0x000E), (0, 19, 0x0FE0, 0xFFC0), (30, 11, 0x07FF, 0xFFF8),
+    (11, 27, 0x7800, 0xF000), (1, 7, 0x00FF, 0x01F8), (8, 23, 0x3E00, 0xFC00),
+    (15, 15, 0x1FFF, 0xFFF0), (31, 31, 0x607F, 0xFFFE), (2, 1, 0x603F, 0xFE06),
+    (24, 17, 0x07E0, 0xFFC0), (19, 9, 0x03FF, 0xFFF0), (18, 25, 0x7C00, 0xF800),
+    (21, 5, 0x001F, 0x003E), (3, 21, 0x1FC0, 0xFE00), (13, 13, 0x07FF, 0xFFF0),
+    (28, 29, 0x701F, 0xFF02), (14, 3, 0x0007, 0x000E), (4, 19, 0x0FC0, 0xFE00),
+    (13, 27, 0x7800, 0xF000), (3, 7, 0x00FF, 0x01F8), (17, 23, 0x3E00, 0xFC00),
+    (26, 15, 0x0FF0, 0xFFE0), (15, 31, 0x6000, 0xC000), (3, 0, 0x603F, 0xFE06),
+    (25, 16, 0x0FE0, 0xFFC0), (29, 8, 0x00FF, 0x01F8), (10, 24, 0x7C00, 0xF800),
+    (24, 4, 0x001F, 0x007C), (29, 20, 0x1FC0, 0xFE00), (20, 12, 0x07FF, 0xFFF0),
+    (25, 28, 0x701F, 0xFFE2), (11, 2, 0x0007, 0x000E), (5, 18, 0x1FC0, 0xFE00),
+    (11, 10, 0x07FF, 0xFFF0), (12, 26, 0x7800, 0xF000), (2, 6, 0x00FF, 0x01F8),
+    (9, 22, 0x3E00, 0xFC00), (31, 14, 0x0180, 0x0300), (30, 30, 0x0003, 0x0006),
+    (7, 0, 0x0003, 0x0006), (27, 16, 0x0FE0, 0xFFC0), (19, 4, 0x0007, 0x000E),
+    (26, 28, 0x700F, 0xFF82), (12, 2, 0x0007, 0x000E), (30, 26, 0x7800, 0xF000),
+    (0, 6, 0x001F, 0x01FC), (5, 1, 0x603F, 0xFE06), (4, 9, 0x00FF, 0x01F8),
+    (22, 5, 0x001F, 0x003E), (31, 21, 0x1F80, 0xFC00), (16, 3, 0x0007, 0x000E),
+    (14, 27, 0x7800, 0xF000), (28, 7, 0x001F, 0x00FC), (16, 31, 0x6000, 0xC000),
+    (0, 1, 0x701F, 0xFE02), (25, 5, 0x000F, 0x001C), (10, 3, 0x0003, 0x0006),
+    (20, 27, 0x7800, 0xF000), (27, 7, 0x001F, 0x0078), (6, 0, 0x0001, 0x0002),
+    (20, 4, 0x0007, 0x000E), (6, 28, 0x7800, 0xF000), (15, 2, 0x0007, 0x000E),
+    (26, 6, 0x000F, 0x007C), (23, 4, 0x0007, 0x000E), (9, 2, 0x0001, 0x0002),
+    (18, 5, 0x0007, 0x000E), (8, 3, 0x0001, 0x0002), (23, 27, 0x7000, 0xE000),
 )
 
 

time: 191 us -> 182 us (0.953)
  the two profiles are of different devices: /device:TPU:386 before, /device:TPU:294 now
where the time goes in v4:
time: 182 us
  Pallas kernels  180 us (99%)
  local copies, waits for them, and re-layouts  2.3 us (1%)
    pallas_call x1, Pallas kernels, local(): pl.pallas_call(functools.partial(kernel, n, cols, slots), out_shape=jax.S...  180 us

profile of v4, /device:TPU:294, one launch (start us, length us, event | category | flops | bytes accessed | tf_op | source)
XLA Modules:
  0.0 182.0 jit_solution(11241452012914347898)
XLA Ops:
  0.0 179.6 %strided_attention.1 = bf16[32,8,2048]{2,1,0:T(8,128)(2,1)} custom-call(bf16[32,8,2048]{2,1,0:T(8,128)(2,1)} %bitcast.5, bf16[32,8,2048]{2,1,0:T(8,128)(2,1)} %bitcast.6, bf16[32,8,2048]{2,1,0:T(8,128)(2,1)} %bitcast.7), custom_call_target="tpu_custom_call" | custom-call | flops 2147483648 | bytes 4194304 | tf_op jit(solution)/shard_map/strided_attention/pallas_call | solution.py:480
  179.6 2.3 %copy.5 = bf16[1,256,2048]{2,1,0:T(8,128)(2,1)} copy(bf16[1,256,2048]{2,1,0:T(8,128)(2,1)} %bitcast.4) | data formatting | bytes 2097152

commit v5 on v3

--- a/solution.py
+++ b/solution.py
@@ -12,42 +12,42 @@
 HD = 128
 FLOOR = -1e30
 POWER = math.log2(math.e) / math.sqrt(HD)
-CHUNK_HEADS = 8
+CHUNK_HEADS = 4
 CHUNKS = HEADS // CHUNK_HEADS
 WIDTH = CHUNK_HEADS * HD
 MESH = pl.DeviceIdType.MESH
 
 ROLES = (
-    (1, 0, 0x701F, 0xFE06), (15, 16, 0x1FFF, 0xFFF0), (27, 8, 0x03FF, 0xFFFE),
-    (21, 24, 0x3FFF, 0xFFE0), (19, 4, 0x41FF, 0xFFFE), (17, 20, 0x7F00, 0xFE00),
-    (30, 12, 0x0FFF, 0xFFFC), (29, 28, 0x701F, 0xFFFE), (11, 2, 0x7FFF, 0xFFFE),
-    (2, 18, 0x1FE0, 0xFFC0), (5, 10, 0x07FF, 0xFFF8), (23, 26, 0x701F, 0xFF06),
-    (22, 6, 0x03FF, 0xFFFE), (8, 22, 0x7FFF, 0xFFE0), (13, 14, 0x1FFF, 0xFFF0),
-    (25, 30, 0x607F, 0xFFFE), (0, 1, 0x701F, 0xFE02), (24, 17, 0x0FF0, 0xFFE0),
-    (28, 9, 0x03FF, 0xFFFE), (18, 25, 0x780F, 0xFFC0), (9, 5, 0x41FF, 0xFFFC),
-    (25, 21, 0x1F80, 0xFF00), (12, 13, 0x07FF, 0xFFF0), (31, 29, 0x603F, 0xFFFE),
-    (10, 3, 0x0007, 0x000E), (0, 19, 0x0FE0, 0xFFC0), (6, 11, 0x07FF, 0xFFF8),
-    (22, 27, 0x7C00, 0xF800), (3, 7, 0x03FF, 0xFFFC), (20, 23, 0x0FFF, 0xFFE0),
-    (14, 15, 0x1FFF, 0xFFF0), (24, 31, 0x700F, 0xFF06), (2, 1, 0x601F, 0xFE06),
+    (0, 0, 0x701F, 0xFE02), (24, 16, 0x0FF0, 0xFFE0), (27, 8, 0x03FF, 0xFFFE),
+    (21, 24, 0x3FFF, 0xFFE0), (19, 4, 0x41FF, 0xFFFE), (31, 20, 0x1FC0, 0xFE00),
+    (30, 12, 0x0FFF, 0xFFFC), (31, 28, 0x603F, 0xFFFE), (11, 2, 0x7FFF, 0xFFFE),
+    (2, 18, 0x1FE0, 0xFFC0), (10, 10, 0x07FF, 0xFFF0), (23, 26, 0x701F, 0xFF06),
+    (3, 6, 0x03FF, 0xFFFC), (8, 22, 0x7FFF, 0xFFE0), (14, 14, 0x1FFF, 0xFFF0),
+    (25, 30, 0x607F, 0xFFFE), (1, 1, 0x701F, 0xFE06), (15, 17, 0x1FFF, 0xFFF0),
+    (4, 9, 0x07FF, 0xFFF8), (18, 25, 0x780F, 0xFFC0), (9, 5, 0x41FF, 0xFFFC),
+    (17, 21, 0x7F00, 0xFE00), (16, 13, 0x07FF, 0xFFF0), (29, 29, 0x701F, 0xFFFE),
+    (12, 3, 0x0007, 0x000E), (1, 19, 0x0FE0, 0xFFC0), (5, 11, 0x07FF, 0xFFF8),
+    (22, 27, 0x7C00, 0xF800), (22, 7, 0x03FF, 0xFFFE), (20, 23, 0x0FFF, 0xFFE0),
+    (13, 15, 0x1FFF, 0xFFF0), (26, 31, 0x603F, 0xFE06), (2, 1, 0x601F, 0xFE06),
     (18, 17, 0x07F0, 0xFFE0), (26, 9, 0x00FF, 0x01F8), (27, 25, 0x7C00, 0xF800),
-    (17, 5, 0x00FF, 0xFFFE), (31, 21, 0x1FC0, 0xFE00), (16, 13, 0x07FF, 0xFFF0),
-    (3, 29, 0x7C00, 0xF800), (12, 3, 0x0007, 0x000E), (1, 19, 0x0FE0, 0xFFC0),
-    (5, 27, 0x7800, 0xF000), (0, 7, 0x001F, 0x01FC), (9, 23, 0x3E00, 0xFC00),
-    (26, 31, 0x603F, 0xFE06), (7, 0, 0x0007, 0x000E), (23, 16, 0x0FE0, 0xFF00),
-    (4, 8, 0x07FF, 0xFFF8), (28, 24, 0x7C00, 0xF800), (18, 4, 0x000F, 0x003E),
-    (26, 20, 0x1FC0, 0xFE00), (29, 12, 0x0060, 0x00C0), (7, 28, 0x603F, 0xFFF0),
-    (15, 2, 0x0007, 0x000E), (7, 18, 0x1FC0, 0xFF80), (10, 10, 0x07FF, 0xFFF0),
-    (6, 26, 0x7800, 0xF000), (23, 6, 0x007F, 0x00F8), (19, 22, 0x3E00, 0xF800),
-    (31, 14, 0x00C0, 0x0180), (4, 30, 0x7800, 0xF000), (4, 0, 0x0003, 0x0006),
-    (20, 4, 0x000F, 0x001E), (19, 20, 0x0200, 0x0400), (30, 28, 0x0001, 0x0002),
-    (8, 2, 0x0001, 0x0002), (29, 18, 0x0FE0, 0xFF00), (16, 26, 0x7800, 0xF000),
-    (2, 6, 0x001F, 0x01F8), (13, 30, 0x6000, 0xC000), (6, 1, 0x0003, 0x0006),
-    (8, 5, 0x000F, 0x001C), (12, 29, 0x7800, 0xF000), (13, 3, 0x0007, 0x000E),
-    (10, 27, 0x7800, 0xF000), (1, 7, 0x001F, 0x01F8), (14, 31, 0x6000, 0xC000),
-    (3, 1, 0x0001, 0x0002), (16, 5, 0x0007, 0x000E), (20, 29, 0x7000, 0xE000),
-    (14, 3, 0x0007, 0x000E), (30, 27, 0x7000, 0xE000), (24, 7, 0x000F, 0x00F8),
-    (21, 31, 0x4000, 0x8000), (5, 0, 0x0003, 0x0006), (21, 4, 0x000F, 0x001E),
-    (9, 2, 0x0001, 0x0002), (15, 30, 0x6000, 0xC000),
+    (17, 5, 0x00FF, 0xFFFE), (26, 21, 0x1FC0, 0xFE00), (29, 13, 0x0060, 0x00C0),
+    (7, 29, 0x603F, 0xFFF0), (14, 3, 0x0007, 0x000E), (7, 19, 0x1FC0, 0xFF80),
+    (6, 11, 0x07FF, 0xFFF8), (5, 27, 0x7800, 0xF000), (23, 7, 0x007F, 0x00F8),
+    (9, 23, 0x3E00, 0xFC00), (24, 31, 0x700F, 0xFF06), (7, 0, 0x0007, 0x000E),
+    (23, 16, 0x0FE0, 0xFF00), (28, 8, 0x03FF, 0xFFFE), (28, 24, 0x7C00, 0xF800),
+    (18, 4, 0x000F, 0x003E), (25, 20, 0x1F80, 0xFF00), (12, 12, 0x07FF, 0xFFF0),
+    (3, 28, 0x7C00, 0xF800), (10, 2, 0x0007, 0x000E), (0, 18, 0x0FE0, 0xFFC0),
+    (10, 26, 0x7800, 0xF000), (0, 6, 0x001F, 0x01FC), (31, 14, 0x00C0, 0x0180),
+    (13, 30, 0x6000, 0xC000), (4, 0, 0x0003, 0x0006), (20, 4, 0x000F, 0x001E),
+    (12, 28, 0x7800, 0xF000), (13, 2, 0x0007, 0x000E), (30, 26, 0x7000, 0xE000),
+    (1, 6, 0x001F, 0x01F8), (14, 30, 0x6000, 0xC000), (5, 1, 0x0003, 0x0006),
+    (8, 5, 0x000F, 0x001C), (19, 21, 0x0200, 0x0400), (30, 29, 0x0001, 0x0002),
+    (15, 3, 0x0007, 0x000E), (29, 19, 0x0FE0, 0xFF00), (6, 27, 0x7800, 0xF000),
+    (2, 7, 0x001F, 0x01F8), (19, 23, 0x3E00, 0xF800), (4, 31, 0x7800, 0xF000),
+    (6, 1, 0x0003, 0x0006), (16, 5, 0x0007, 0x000E), (8, 3, 0x0001, 0x0002),
+    (16, 27, 0x7800, 0xF000), (24, 7, 0x000F, 0x00F8), (15, 31, 0x6000, 0xC000),
+    (3, 0, 0x0001, 0x0002), (21, 4, 0x000F, 0x001E), (20, 28, 0x7000, 0xE000),
+    (9, 2, 0x0001, 0x0002), (21, 30, 0x4000, 0x8000),
 )
 
 

time: 191 us -> 184 us (0.963)
  the two profiles are of different devices: /device:TPU:386 before, /device:TPU:388 now
where the time goes in v5:
time: 184 us
  Pallas kernels  181 us (98%)
  local copies, waits for them, and re-layouts  2.3 us (1%)
    pallas_call x1, Pallas kernels, local(): pl.pallas_call(functools.partial(kernel, n, cols, slots), out_shape=jax.S...  181 us

profile of v5, /device:TPU:388, one launch (start us, length us, event | category | flops | bytes accessed | tf_op | source)
XLA Modules:
  0.0 183.6 jit_solution(11914214054103485714)
XLA Ops:
  0.0 181.3 %strided_attention.1 = bf16[32,8,2048]{2,1,0:T(8,128)(2,1)} custom-call(bf16[32,8,2048]{2,1,0:T(8,128)(2,1)} %bitcast.5, bf16[32,8,2048]{2,1,0:T(8,128)(2,1)} %bitcast.6, bf16[32,8,2048]{2,1,0:T(8,128)(2,1)} %bitcast.7), custom_call_target="tpu_custom_call" | custom-call | flops 2147483648 | bytes 4194304 | tf_op jit(solution)/shard_map/strided_attention/pallas_call | solution.py:479
  181.3 2.3 %copy.5 = bf16[1,256,2048]{2,1,0:T(8,128)(2,1)} copy(bf16[1,256,2048]{2,1,0:T(8,128)(2,1)} %bitcast.4) | data formatting | bytes 2097152
